TPU v7x, 256 devices: a whole 4x4x8 slice. The times are simulated.
256 devices in a mesh: ctx: 64 (over y, z_hi, x, core), hg: 4 (over z_lo).
Axes of the slice: x: 4, y: 4, z: 8 (z_hi: 2, z_lo: 4; z = z_hi * 4 + z_lo), core: 2. Of those that a mesh axis runs over, the one named last changes fastest.
Arguments:
- main_query: bfloat16 [256, 24576], P('ctx', 'hg'), may hold values from -120 to 120
- index_query: bfloat16 [256, 8192], P('ctx', 'hg'), may hold values from -8 to 8
- index_weight: bfloat16 [256, 64], P('ctx', 'hg'), may hold values from 0.099609375 to 1
- main_nope: bfloat16 [65536, 16384], P('ctx', 'hg'), may hold values from -6 to 6
- main_rope: bfloat16 [65536, 64], P('ctx'), may hold values from -6 to 6
- index_keys: bfloat16 [65536, 128], P('ctx'), may hold values from -6 to 6
- query_pos: int32 [256], replicated, may hold values from 0 to 65535, as said below
- query_seg: int32 [256], replicated, may hold values from 0 to 7, as said below
- key_pos: int32 [65536], P('ctx'), may hold values from 0 to 65535, as said below
- key_seg: int32 [65536], P('ctx'), may hold values from 0 to 7, as said below
- loss_weight: float32 [256], replicated, may hold values from 4 to 40
Outputs:
- index_query_grad: float32 [256, 8192], P('ctx', 'hg')
- index_key_grad: float32 [65536, 128], P('ctx')
- query_loss: float32 [256], P('hg')
Inputs may be any that keep to these rules, and one draw needn't show every extreme that they name: `key_pos`: a permutation of the positions 0 to 65535. `query_pos`: 256 distinct positions below 65536, among them 0 and 65535. `key_seg`: documents are runs of consecutive positions numbered from 0 upward, max(8, 2) of them; the document of the key at that position. `query_seg`: the document of the query's position, numbered as for key_seg.
All inputs are finite; a program needn't handle non-finite values.
Results may differ from a plain program's by a relative error of at most 0.007.
Values may be sent and summed in bfloat16 or wider, within the bound.
A program may use at most 192 MiB of HBM per device.

v0:
```python
import math

import jax
import jax.numpy as jnp
from jax import lax
from jax.sharding import PartitionSpec as P

H = 128
DN = 128
DI = 128
QK = 192


def index_loss(target, logits, allowed, weight):
    masked = jnp.where(allowed, logits, jnp.float32(-1e30))
    local_peak = jnp.max(masked, axis=1)
    cross_part = jnp.sum(target * logits, axis=1)
    peak = lax.pmax(local_peak, "ctx")
    local_total = jnp.sum(jnp.where(allowed, jnp.exp(masked - peak[:, None]), 0.0), axis=1)
    total, cross = lax.psum((local_total, cross_part), "ctx")
    log_norm = peak + jnp.log(total)
    row_loss = weight * (log_norm - cross)
    dlogit = weight[:, None] * (
        jnp.where(allowed, jnp.exp(logits - log_norm[:, None]), 0.0) - target
    )
    return (dlogit, row_loss)


def per_device(
    main_query,
    index_query,
    index_weight,
    main_nope,
    main_rope,
    index_keys,
    query_pos,
    query_seg,
    key_pos,
    key_seg,
    loss_weight,
):
    heads = main_nope.shape[1] // DN
    index_heads = index_weight.shape[1]
    own_rows = main_query.shape[0]
    every_query, every_index, every_weight = (
        lax.all_gather(main_query, "ctx", axis=0, tiled=True),
        lax.all_gather(index_query, "ctx", axis=0, tiled=True),
        lax.all_gather(index_weight, "ctx", axis=0, tiled=True),
    )
    rows = every_query.shape[0]
    keys = main_nope.shape[0]
    allowed = (key_pos[None, :] <= query_pos[:, None]) & (key_seg[None, :] == query_seg[:, None])
    shaped = every_query.reshape(rows, heads, QK)
    plain_keys = main_nope.reshape(keys, heads, DN)
    scores = jnp.einsum(
        "qhd,khd->hqk", shaped[:, :, :DN], plain_keys, preferred_element_type=jnp.float32
    )
    scores = scores + jnp.einsum(
        "qhd,kd->hqk", shaped[:, :, DN:], main_rope, preferred_element_type=jnp.float32
    )
    scores = scores / math.sqrt(QK)
    masked = jnp.where(allowed[None], scores, jnp.float32(-1e30))
    local_peak = jnp.max(masked, axis=2)
    peak = lax.pmax(local_peak.astype(jnp.bfloat16), "ctx").astype(local_peak.dtype)
    local_total = jnp.sum(jnp.where(allowed[None], jnp.exp(masked - peak[:, :, None]), 0.0), axis=2)
    total = lax.psum(local_total, "ctx")
    expo = jnp.where(allowed[None], jnp.exp(masked - peak[:, :, None]), 0.0)
    probs = jnp.sum(expo / total[:, :, None], axis=0)
    index_shaped = every_index.reshape(rows, index_heads, DI)
    dots = jnp.einsum("qhd,kd->hqk", index_shaped, index_keys, preferred_element_type=jnp.float32)
    weight_cols = every_weight.astype(jnp.float32).T[:, :, None]
    logit_part = jnp.sum(weight_cols * jnp.maximum(dots, 0.0), axis=0) / math.sqrt(DI)
    share = rows // lax.axis_size("hg")
    offset = lax.axis_index("hg") * share
    prob_sum, logits = lax.psum((probs, logit_part), "hg")
    dlogit, full_loss = index_loss(prob_sum / H, logits, allowed, loss_weight)
    query_loss = lax.dynamic_slice_in_dim(full_loss, offset, share, 0)
    dscore = (dlogit[None] * weight_cols * (dots > 0).astype(jnp.float32) / math.sqrt(DI)).astype(
        jnp.bfloat16
    )
    term = jnp.einsum("hqk,kd->qhd", dscore, index_keys, preferred_element_type=jnp.float32)
    index_query_grad = lax.psum_scatter(
        term.reshape(lax.axis_size("ctx") * own_rows, index_heads * DI),
        "ctx",
        scatter_dimension=0,
        tiled=True,
    )
    key_part = jnp.einsum("hqk,qhd->kd", dscore, index_shaped, preferred_element_type=jnp.float32)
    index_key_grad = lax.psum(key_part, "hg")
    return (index_query_grad, index_key_grad, query_loss)


def solution(mesh):
    return jax.shard_map(
        per_device,
        mesh=mesh,
        in_specs=(
            P("ctx", "hg"),
            P("ctx", "hg"),
            P("ctx", "hg"),
            P("ctx", "hg"),
            P("ctx", None),
            P("ctx", None),
            P(),
            P(),
            P("ctx"),
            P("ctx"),
            P(),
        ),
        out_specs=(P("ctx", "hg"), P("ctx", None), P("hg")),
        check_vma=False,
    )
```

profile of v0, /device:TPU:1, one launch (start us, length us, event | category | flops | bytes accessed | tf_op | source)
XLA Modules:
  0.0 2425.1 jit_solution(11656925121456052773)
XLA Ops:
  10.8 120.8 %all-gather.1 = bf16[64,4,16]{2,1,0:T(4,128)(2,1)S(1)} all-gather(bf16[1,4,16]{2,1,0:T(4,128)(2,1)} %bitcast.53), channel_id=1, replica_groups=mesh['ctx'=64,'hg'=4] {'ctx'}, dimensions={0}, use_global_device_ids=true | all-gather | bytes 8320 | tf_op jit(solution)/shard_map/all_gather | solution.py:48
  131.7 1.8 reshape.76
  133.5 7.2 fusion.3
  141.8 37.7 %all-gather.8.cloned.1.call-done = bf16[64,4,6144]{2,1,0:T(4,128)(2,1)} async-done(((bf16[1,4,6144]{2,1,0:T(4,128)(2,1)}), bf16[64,4,6144]{2,1,0:T(4,128)(2,1)}) %all-gather.8.cloned.1.call-update) | async-done | bytes 3145744 | tf_op jit(solution)/shard_map/all_gather | solution.py:46
  179.4 8.1 reshape.77
  187.6 3.2 slice.8
  190.8 17.2 fusion.4
  208.0 23.2 fusion.17
  231.2 390.1 %pmax.15 = bf16[32,256]{1,0:T(8,128)(2,1)S(1)} all-reduce(bf16[32,256]{1,0:T(8,128)(2,1)} %get-tuple-element.13), channel_id=1, replica_groups=mesh['ctx'=64,'hg'=4] {'ctx'}, use_global_device_ids=true, to_apply=%region_7.8 | all-reduce | flops 8192 | bytes 32768 | tf_op jit(solution)/shard_map/pmax | solution.py:64
  621.3 15.6 fusion.2
  636.9 400.1 %psum.44 = f32[32,256]{1,0:T(8,128)S(1)} all-reduce(f32[32,256]{1,0:T(8,128)S(1)} %fusion.2), channel_id=1, replica_groups=mesh['ctx'=64,'hg'=4] {'ctx'}, use_global_device_ids=true, to_apply=%region_9.10 | all-reduce | flops 8192 | bytes 65536 | tf_op jit(solution)/shard_map/psum | solution.py:66
  1037.1 14.5 divide_reduce_fusion
  1053.0 103.3 %all-reduce.11.cloned.1.call-done = (f32[256,1024]{0,1:T(8,128)}, f32[256,1024]{0,1:T(8,128)}) async-done(((f32[256,1024]{0,1:T(8,128)}, f32[256,1024]{0,1:T(8,128)}), (f32[256,1024]{0,1:T(8,128)}, f32[256,1024]{0,1:T(8,128)})) %all-reduce.11.cloned.1.call-update) | async-done | bytes 2097168 | tf_op jit(solution)/shard_map/psum | solution.py:75
  1156.3 1.6 fusion.12
  1157.9 201.2 %pmax.14 = f32[256]{0:T(256)S(1)} all-reduce(f32[256]{0:T(256)S(1)} %fusion.12), channel_id=1, replica_groups=mesh['ctx'=64,'hg'=4] {'ctx'}, use_global_device_ids=true, to_apply=%region_3.4 | all-reduce | flops 256 | bytes 2048 | tf_op jit(solution)/shard_map/pmax | solution.py:18
  1359.1 1.9 multiply_reduce_fusion
  1361.0 208.9 %all-reduce.1 = (f32[256]{0:T(256)S(1)}, f32[256]{0:T(256)S(1)}) all-reduce(f32[256]{0:T(256)S(1)} %get-tuple-element.4, f32[256]{0:T(256)S(1)} %get-tuple-element.3), channel_id=1, replica_groups=mesh['ctx'=64,'hg'=4] {'ctx'}, use_global_device_ids=true, to_apply=%region_5.6 | all-reduce | flops 512 | bytes 4096 | tf_op jit(solution)/shard_map/psum | solution.py:20
  1569.8 2.0 subtract_multiply_fusion
  1572.8 7.4 fusion.13
  1580.2 1.8 copy.54
  1582.2 9.6 convolution_bitcast_fusion
  1593.6 769.3 %all-reduce.9.cloned.1.call-done = f32[256,2048]{1,0:T(8,128)} async-done(((f32[256,2048]{1,0:T(8,128)}), f32[256,2048]{1,0:T(8,128)}) %all-reduce.9.cloned.1.call-update) | async-done | bytes 2097168
  2364.4 52.3 %all-reduce.7.cloned.1.call-done = f32[1024,128]{1,0:T(8,128)} async-done(((f32[1024,128]{1,0:T(8,128)}), f32[1024,128]{1,0:T(8,128)}) %all-reduce.7.cloned.1.call-update) | async-done | bytes 524304 | tf_op jit(solution)/shard_map/psum | solution.py:89
  2416.7 1.9 copy.83
  (43 shorter events, 9.9 us)
Async XLA Ops:
  7.2 126.3 %copy-start = (bf16[1024,128]{1,0:T(8,128)(2,1)S(1)}, bf16[1024,128]{1,0:T(8,128)(2,1)}, u32[]{:S(2)}) copy-start(bf16[1024,128]{1,0:T(8,128)(2,1)} %param.16) | copy-start | bytes 786436
  7.2 124.5 %all-gather.6.cloned.1.call-start = ((), (), s32[]{:S(2)}) async-start(), calls=%async_computation.1 | async-start | bytes 1064960 | tf_op jit(solution)/shard_map/all_gather | solution.py:47
  7.9 171.5 %all-gather.8.cloned.1.call-start = ((), (), s32[]{:S(2)}) async-start(), calls=%async_computation.2 | async-start | bytes 3194880 | tf_op jit(solution)/shard_map/all_gather | solution.py:46
  8.7 1147.6 %all-reduce.11.cloned.1.call-start = ((), (), s32[]{:S(2)}) async-start(), calls=%async_computation.4 | async-start | bytes 4194304 | tf_op jit(solution)/shard_map/psum | solution.py:75
  190.8 17.2 slice-start
  190.8 17.2 copy-start.3
  621.3 415.7 %copy-start.1 = (pred[256,1024]{1,0:T(8,128)(4,1)S(1)}, pred[256,1024]{1,0:T(8,128)(4,1)}, u32[]{:S(2)}) copy-start(pred[256,1024]{1,0:T(8,128)(4,1)} %copy.46) | copy-start | bytes 786436
  1037.0 119.3 %copy-start.4 = (s32[1024]{0:T(1024)S(1)}, s32[1024]{0:T(1024)}, u32[]{:S(2)}) copy-start(s32[1024]{0:T(1024)} %param.20) | copy-start | bytes 12292
  1037.0 119.3 %copy-start.5 = (s32[1024]{0:T(1024)S(1)}, s32[1024]{0:T(1024)}, u32[]{:S(2)}) copy-start(s32[1024]{0:T(1024)} %param.19) | copy-start | bytes 12292
  1037.0 119.3 %copy-start.6 = (s32[256]{0:T(256)S(1)}, s32[256]{0:T(256)}, u32[]{:S(2)}) copy-start(s32[256]{0:T(256)} %param.18) | copy-start | bytes 3076
  1037.0 119.3 %copy-start.7 = (s32[256]{0:T(256)S(1)}, s32[256]{0:T(256)}, u32[]{:S(2)}) copy-start(s32[256]{0:T(256)} %param.17) | copy-start | bytes 3076
  1037.0 532.8 %copy-start.8 = (f32[256]{0:T(256)S(1)}, f32[256]{0:T(256)}, u32[]{:S(2)}) copy-start(f32[256]{0:T(256)} %param.21) | copy-start | bytes 3076
  1052.9 1310.0 %all-reduce.9.cloned.1.call-start = ((), (), s32[]{:S(2)}) async-start(), calls=%async_computation.3 | async-start | bytes 4194304
  1571.8 1.0 copy-start.2
  1582.1 9.7 copy-start.9
  1582.1 834.6 %all-reduce.7.cloned.1.call-start = ((), (), s32[]{:S(2)}) async-start(), calls=%async_computation | async-start | bytes 1048576 | tf_op jit(solution)/shard_map/psum | solution.py:89
Sparse Core Ops, SparseCore 0:
  11.6 82.6 all-gather.5
  98.0 81.4 all-gather.7
  1053.1 103.1 all-reduce.10
  1582.2 780.6 all-reduce.8
  2366.0 50.6 all-reduce.6
where the time goes:
time: 2430 us
  blocking collectives  1320 us (54%)
  waiting for transfers between devices  964 us (40%)
  matrix products  64.6 us (3%)
  other arithmetic  37.7 us (2%)
    unnamed x6, waiting for transfers between devices  771 us
    psum x1, blocking collectives, per_device(): total = lax.psum(local_total, 'ctx')  400 us
    pmax x1, blocking collectives, per_device(): lax.pmax(local_peak.astype(jnp.bfloat16), 'ctx').astype(local_peak.dtype)  390 us
    psum x1, blocking collectives, index_loss(): total, cross = lax.psum((local_total, cross_part), 'ctx')  209 us
    pmax x1, blocking collectives, index_loss(): peak = lax.pmax(local_peak, 'ctx')  201 us
    all_gather x1, blocking collectives, per_device(): lax.all_gather(index_weight, 'ctx', axis=0, tiled=True)  121 us
    psum x1, waiting for transfers between devices, per_device(): prob_sum, logits = lax.psum((probs, logit_part), 'hg')  103 us
    psum x1, waiting for transfers between devices, per_device(): index_key_grad = lax.psum(key_part, 'hg')  52.3 us
  transfers between devices with their start and end apart: 5, of which 4 were waited for; matrix products, arithmetic and copies ran while one was open for 1% of the time, Pallas kernels for 0%

commit v1 on v0

v1 whole, which is shorter than its diff:
```python
import functools
import math

import jax
import jax.numpy as jnp
from jax import lax
from jax.experimental import pallas as pl
from jax.experimental.pallas import tpu as pltpu
from jax.sharding import PartitionSpec as P

MESH = pl.DeviceIdType.MESH
F32 = jnp.float32
BF16 = jnp.bfloat16
DN = 128
DR = 64
DI = 128
QK = 192
H = 128
QN = 256
KEYS = 1024
BLK = 256
IC = 512
MC = 1536
CW = IC + MC + 128
HEADS = 32
LOG2E = math.log2(math.e)
NEG = -1e30

S_GROUP, S_Z, S_R1, S_R2, S_SIB = 0, 3, 4, 8, 24
S_LOGIT, S_LN, S_LSE, S_PROB, S_DL, S_CROSS = 40, 43, 46, 54, 57, 60
S_KRS, S_KAG, S_GSIB, S_GREL, S_GR1, S_GR2, S_GZ, S_GGRP = 71, 74, 77, 79, 83, 91, 94, 95
N_SEM = 98


def dot_tt(a, b):
    return lax.dot_general(a, b, (((1,), (1,)), ((), ())), preferred_element_type=F32)


def dot_nn(a, b):
    return lax.dot_general(a, b, (((1,), (0,)), ((), ())), preferred_element_type=F32)


def kernel(
    pack_ref, ik_ref, rope_ref, kcode_ref, qv_ref, lw_ref, nope_hbm,
    oq_ref, ok_ref, oloss_ref,
    ssem, rsem, lsem,
    gbuf, gasm, G, KV, bias, W, KT, L, LB, LQ, LNS, LNB,
    E, M, SUM, XS, XSIB, XX, XY, XZ, PS, PB, TQ, DL, CS, CHG, CSIB, CX, CY, CZ,
    KA, KS, KB, KG, T, RB, U, RL, RR, V, VB, VZ, YB, OB,
):
    me = lax.axis_index("ctx")
    hg = lax.axis_index("hg")
    c = lax.rem(me, 2)
    x = lax.rem(me // 2, 4)
    z = lax.rem(me // 8, 2)
    y = me // 16
    xb, xp = lax.rem(x, 2), x // 2
    q = xb * 2 + c
    first = c == 0

    def cid(yy, zz, xx, cc):
        return ((yy * 2 + zz) * 4 + xx) * 2 + cc

    def mod4(v):
        return lax.rem(v + 4, 4)

    sib = (cid(y, z, x, 1 - c), hg)
    xo = x + 1 - 2 * xb
    group = [
        (xb * 2 + 1 - c, sib),
        ((1 - xb) * 2 + c, (cid(y, z, xo, c), hg)),
        ((1 - xb) * 2 + 1 - c, (cid(y, z, xo, 1 - c), hg)),
    ]
    zdev = (cid(y, 1 - z, x, c), hg)
    xdev = {s: (cid(y, z, mod4(x + s), c), hg) for s in (1, -1, 2)}
    ydev = {s: (cid(mod4(y + s), z, x, c), hg) for s in (1, -1, 2)}
    hdev = {s: (me, mod4(hg + s)) for s in (1, 2, 3)}
    r1 = {s: (jnp.where(first, xdev[s][0], ydev[s][0]), hg) for s in (1, -1, 2)}
    r2 = {s: (jnp.where(first, ydev[s][0], xdev[s][0]), hg) for s in (1, -1, 2)}

    started = []

    def send(src, dst, k, dev):
        cp = pltpu.make_async_remote_copy(
            src_ref=src, dst_ref=dst, send_sem=ssem.at[k], recv_sem=rsem.at[k],
            device_id=dev, device_id_type=MESH,
        )
        cp.start()
        started.append(cp)
        return cp

    loads = []
    for i in range(4):
        cols = pl.ds(i * 1024, 1024)
        cp = pltpu.make_async_copy(nope_hbm.at[:, cols], KV.at[:, cols], lsem.at[i])
        cp.start()
        loads.append(cp)

    barrier = pltpu.get_barrier_semaphore()
    partners = [sib, group[1][1], group[2][1], zdev, xdev[2], hdev[1], hdev[2], hdev[3]]
    partners += [ydev[s] for s in (1, -1, 2)]
    xn = (cid(y, z, mod4(x - 1 + 2 * xb), c), hg)
    partners.append(xn)
    for dev in partners:
        pl.semaphore_signal(barrier, inc=1, device_id=dev, device_id_type=MESH)
    pl.semaphore_wait(barrier, len(partners))

    cps = [
        send(pack_ref.at[g], gbuf.at[q], S_GROUP + i, dev) for i, (g, dev) in enumerate(group)
    ]
    gbuf[q] = pack_ref[q]

    kcode = kcode_ref[...]
    ok = (kcode >= qv_ref[0:1, :]) & (kcode <= qv_ref[1:2, :])
    bias[...] = jnp.where(ok, 0.0, NEG).astype(F32)
    KT[...] = jnp.transpose(ik_ref[...].astype(F32)).astype(BF16)

    for cp in cps:
        cp.wait_recv()
    for s in range(4):
        gasm[4 * s : 4 * s + 4, :] = gbuf[s]

    def unit(ch, yy, xx):
        return G.at[ch, pl.ds(pl.multiple_of((yy * 2 + xx) * 32, 32), 32), :]

    def half(ch, yy, xx, zz):
        return G.at[ch, pl.ds(pl.multiple_of(((yy * 2 + xx) * 2 + zz) * 16, 16), 16), :]

    own_rows = pl.multiple_of(((y * 2 + xp) * 2 + z) * 16, 16)
    G[q, pl.ds(own_rows, 16), :] = gasm[...].astype(BF16)
    own_half = half(q, y, xp, z)
    cpz = send(own_half, own_half, S_Z, zdev)

    def r1_coord(s):
        xx, yy = mod4(x + s), mod4(y + s)
        return (
            jnp.where(first, lax.rem(xx, 2) * 2 + c, q),
            jnp.where(first, y, yy),
            jnp.where(first, xx // 2, xp),
        )

    def r2_coord(s, k):
        xx = jnp.where(first, mod4(x + k), mod4(x + s))
        yy = jnp.where(first, mod4(y + s), mod4(y + k))
        return (lax.rem(xx, 2) * 2 + c, yy, xx // 2)

    sib_cps = []

    def to_sib(co):
        u = unit(*co)
        sib_cps.append(send(u, u, S_SIB + len(sib_cps), sib))

    offs = (0, -1, 1, 2)
    r2p, r2m = {}, {}

    def to_r2(k):
        u = unit(*r1_coord(offs[k]))
        r2p[k] = send(u, u, S_R2 + k, r2[1])
        r2m[k] = send(u, u, S_R2 + 4 + k, r2[-1])

    cpz.wait_recv()
    cpz.wait_send()
    u0 = unit(*r1_coord(0))
    cp_p = send(u0, u0, S_R1, r1[1])
    cp_m = send(u0, u0, S_R1 + 1, r1[-1])
    to_r2(0)
    to_sib(r1_coord(0))
    cp_p.wait_recv()
    h = half(*r1_coord(-1), 0)
    cp_fp = send(h, h, S_R1 + 2, r1[1])
    to_r2(1)
    cp_m.wait_recv()
    h = half(*r1_coord(1), 1)
    cp_fm = send(h, h, S_R1 + 3, r1[-1])
    to_r2(2)
    to_sib(r1_coord(-1))
    to_sib(r1_coord(1))
    cp_fp.wait_recv()
    cp_fm.wait_recv()
    to_r2(3)
    to_sib(r1_coord(2))
    fwd = []
    for k in range(4):
        r2p[k].wait_recv()
        co = r2_coord(-1, offs[k])
        if k < 2:
            fwd.append(send(unit(*co), unit(*co), S_R2 + 8 + k, r2[1]))
        to_sib(co)
        r2m[k].wait_recv()
        co = r2_coord(1, offs[k])
        if k >= 2:
            fwd.append(send(unit(*co), unit(*co), S_R2 + 8 + k, r2[-1]))
        to_sib(co)
    for k in range(4):
        fwd[k].wait_recv()
        to_sib(r2_coord(2, offs[k]))
    for cp in sib_cps:
        cp.wait_recv()

    def index_chunk(ch, carry):
        w = jnp.transpose(G[ch, :, IC + MC : CW].astype(F32))
        W[ch] = w[0:8, :] * (1.0 / math.sqrt(DI))
        for b in range(4):
            acc = jnp.zeros((BLK, QN), F32)
            for j in range(4):
                d = dot_tt(ik_ref[b * BLK : (b + 1) * BLK, :], G[ch, :, j * DI : (j + 1) * DI])
                acc = acc + jnp.maximum(d, 0.0) * W[ch, j : j + 1, :]
            L[b] = L[b] + acc
        return carry

    L[...] = jnp.zeros(L.shape, F32)
    lax.fori_loop(0, 4, index_chunk, 0)
    lcps = [send(L.at[mod4(hg + s)], LB.at[s - 1], S_LOGIT + s - 1, hdev[s]) for s in (1, 2, 3)]

    for cp in loads:
        cp.wait()

    scale = LOG2E / math.sqrt(QK)

    def main_pair(p, carry):
        ch = p // 4
        off = IC + lax.rem(p, 4) * 384
        qr = G[ch, :, pl.ds(pl.multiple_of(off + 256, 128), 128)]
        for i in range(2):
            hd = 2 * p + i
            qn = G[ch, :, pl.ds(pl.multiple_of(off + i * 128, 128), 128)]
            rhs = jnp.concatenate([qn, qr], axis=1)
            kcols = pl.ds(pl.multiple_of(hd * DN, 128), DN)
            for b in range(4):
                rows = slice(b * BLK, (b + 1) * BLK)
                lhs = jnp.concatenate(
                    [KV[rows, kcols], rope_ref[rows, i * 128 : (i + 1) * 128]], axis=1
                )
                s = dot_tt(lhs, rhs) * scale + bias[rows, :]
                m = jnp.max(s, axis=0, keepdims=True)
                e = jnp.exp2(s - m)
                M[b, pl.ds(hd, 1), :] = m
                SUM[b, pl.ds(hd, 1), :] = jnp.sum(e, axis=0, keepdims=True)
                E[hd, rows, :] = e.astype(BF16)
        return carry

    lax.fori_loop(0, 8, main_pair, 0)

    for cp in lcps:
        cp.wait_recv()
    lq = L[hg] + LB[0] + LB[1] + LB[2]
    LQ[...] = lq
    qrows = pl.ds(pl.multiple_of(hg * BLK, BLK), BLK)
    l2 = lq * LOG2E + bias[qrows, :]
    m = jnp.max(l2, axis=0, keepdims=True)
    part = m + jnp.log2(jnp.sum(jnp.exp2(l2 - m), axis=0, keepdims=True))
    LNS[...] = jnp.broadcast_to(part, (8, QN))
    ncps = [send(LNS, LNB.at[s - 1], S_LN + s - 1, hdev[s]) for s in (1, 2, 3)]

    lax.fori_loop(8, 16, main_pair, 0)

    def lse(parts):
        top = functools.reduce(jnp.maximum, parts)
        tot = functools.reduce(jnp.add, [jnp.exp2(v - top) for v in parts])
        return top + jnp.log2(tot)

    mm = jnp.maximum(jnp.maximum(M[0], M[1]), jnp.maximum(M[2], M[3]))
    ss = sum(SUM[b] * jnp.exp2(M[b] - mm) for b in range(4))
    XS[0, 0:HEADS, :] = mm + jnp.log2(ss)
    for cp in ncps:
        cp.wait_recv()
    XS[0, HEADS : HEADS + 8, :] = lse([LNS[...], LNB[0], LNB[1], LNB[2]])

    cp = send(XS.at[0], XSIB, S_LSE, sib)
    cp.wait_recv()
    XS[1] = lse([XS[0], XSIB[...]])
    cps = [send(XS.at[1], XX.at[i], S_LSE + 1 + i, xdev[s]) for i, s in enumerate((1, -1, 2))]
    for cp in cps:
        cp.wait_recv()
    XS[2] = lse([XS[1], XX[0], XX[1], XX[2]])
    cps = [send(XS.at[2], XY.at[i], S_LSE + 4 + i, ydev[s]) for i, s in enumerate((1, -1, 2))]
    for cp in cps:
        cp.wait_recv()
    XS[3] = lse([XS[2], XY[0], XY[1], XY[2]])
    cp = send(XS.at[3], XZ, S_LSE + 7, zdev)
    cp.wait_recv()
    XS[4] = lse([XS[3], XZ[...]])

    for b in range(4):
        M[b] = jnp.exp2(M[b] - XS[4, 0:HEADS, :])

    def head_sum(t, put):
        def sub(i, carry):
            rows = pl.ds(pl.multiple_of(t * BLK + i * 64, 64), 64)
            acc = jnp.zeros((64, QN), F32)
            for hd in range(HEADS):
                acc = acc + E[hd, rows, :].astype(F32) * M[t, hd : hd + 1, :]
            put(pl.ds(pl.multiple_of(i * 64, 64), 64), acc)
            return carry

        lax.fori_loop(0, 4, sub, 0)

    pcps = []
    for s in (1, 2, 3):
        t = mod4(hg + s)

        def put_out(rows, acc, t=t):
            PS[t, rows, :] = acc.astype(BF16)

        head_sum(t, put_out)
        pcps.append(send(PS.at[t], PB.at[s - 1], S_PROB + s - 1, hdev[s]))

    def put_own(rows, acc):
        TQ[rows, :] = acc

    head_sum(hg, put_own)
    for cp in pcps:
        cp.wait_recv()

    target = (
        TQ[...] + PB[0].astype(F32) + PB[1].astype(F32) + PB[2].astype(F32)
    ) * (1.0 / H)
    norm2 = XS[4, HEADS : HEADS + 1, :]
    lq = LQ[...]
    prob = jnp.exp2(lq * LOG2E + bias[qrows, :] - norm2)
    DL[hg] = (lw_ref[0:1, :] * (prob - target)).astype(BF16)
    dcps = [send(DL.at[hg], DL.at[hg], S_DL + s - 1, hdev[s]) for s in (1, 2, 3)]
    cross = jnp.sum(target * lq, axis=0, keepdims=True)
    CS[0] = jnp.broadcast_to(cross, (8, QN))
    ccps = [send(CS.at[0], CHG.at[s - 1], S_CROSS + s - 1, hdev[s]) for s in (1, 2, 3)]
    for cp in ccps + dcps:
        cp.wait_recv()
    CS[1] = CS[0] + CHG[0] + CHG[1] + CHG[2]
    cp_c = send(CS.at[1], CSIB, S_CROSS + 3, sib)

    KA[...] = jnp.zeros(KA.shape, F32)

    def grad_chunk(ch, carry):
        for j in range(4):
            qj = G[ch, :, j * DI : (j + 1) * DI]
            wj = W[ch, j : j + 1, :]
            tt = jnp.zeros((DI, QN), F32)
            for b in range(4):
                d = dot_tt(ik_ref[b * BLK : (b + 1) * BLK, :], qj)
                ds = jnp.where(d > 0, DL[b].astype(F32) * wj, 0.0).astype(BF16)
                KA[b] = KA[b] + dot_nn(ds, qj)
                tt = tt + dot_nn(KT[:, b * BLK : (b + 1) * BLK], ds)
            T[ch, :, j * DI : (j + 1) * DI] = jnp.transpose(tt)
        return carry

    lax.fori_loop(0, 4, grad_chunk, 0)

    KS[...] = KA[...].astype(BF16)
    kcps = [send(KS.at[mod4(hg + s)], KB.at[s - 1], S_KRS + s - 1, hdev[s]) for s in (1, 2, 3)]
    gcps = [send(T.at[2 * k + 1 - c], RB.at[k], S_GSIB + k, sib) for k in range(2)]

    cp_c.wait_recv()
    CS[2] = CS[1] + CSIB[...]
    ccps = [send(CS.at[2], CX.at[i], S_CROSS + 4 + i, xdev[s]) for i, s in enumerate((1, -1, 2))]

    for k in range(2):
        gcps[k].wait_recv()
        U[k] = T[2 * k + c] + RB[k]

    def uref(s, k):
        xx = jnp.where(first, k, mod4(x + s))
        yy = jnp.where(first, mod4(y + s), k)
        return U.at[
            lax.rem(xx, 2), pl.ds(pl.multiple_of((yy * 2 + xx // 2) * 32, 32), 32), :
        ]

    rel = [
        send(uref(2, k), RL.at[k], S_GREL + k, r2[1] if k < 2 else r2[-1]) for k in range(4)
    ]
    for cp in ccps:
        cp.wait_recv()
    CS[3] = CS[2] + CX[0] + CX[1] + CX[2]
    ccps = [send(CS.at[3], CY.at[i], S_CROSS + 7 + i, ydev[s]) for i, s in enumerate((1, -1, 2))]

    rp = [send(uref(1, k), RR.at[0, k], S_GR1 + k, r2[1]) for k in (2, 3)]
    rm = [send(uref(-1, k), RR.at[1, k], S_GR1 + 4 + k, r2[-1]) for k in (0, 1)]
    for k in range(4):
        rel[k].wait_recv()
        u = uref(1 if k < 2 else -1, k)
        u[...] = u[...] + RL[k]
        if k < 2:
            rp.append(send(u, RR.at[0, k], S_GR1 + k, r2[1]))
        else:
            rm.append(send(u, RR.at[1, k], S_GR1 + 4 + k, r2[-1]))

    for cp in kcps:
        cp.wait_recv()
    KG[hg] = KA[hg] + KB[0].astype(F32) + KB[1].astype(F32) + KB[2].astype(F32)
    kcps = [send(KG.at[hg], KG.at[hg], S_KAG + s - 1, hdev[s]) for s in (1, 2, 3)]

    for cp in ccps:
        cp.wait_recv()
    CS[4] = CS[3] + CY[0] + CY[1] + CY[2]
    cp_c = send(CS.at[4], CZ, S_CROSS + 10, zdev)

    for cp in rp + rm:
        cp.wait_recv()
    for k in range(4):
        V[k] = uref(0, k)[...] + RR[0, k] + RR[1, k]

    me1 = jnp.where(first, x, y)
    cps = [
        send(V.at[mod4(me1 + s)], VB.at[i], S_GR2 + i, r1[s]) for i, s in enumerate((1, -1, 2))
    ]
    for cp in cps:
        cp.wait_recv()
    VZ[0] = V[me1] + VB[0] + VB[1] + VB[2]
    cp = send(
        VZ.at[0, pl.ds(pl.multiple_of((1 - z) * 16, 16), 16), :], VZ.at[1, 0:16, :], S_GZ, zdev
    )
    cp_c.wait_recv()
    tot = CS[4] + CZ[...]
    oloss_ref[...] = lw_ref[...] * (
        XS[4, HEADS : HEADS + 8, :] * (1.0 / LOG2E) - tot
    )
    cp.wait_recv()
    own = VZ[0, pl.ds(pl.multiple_of(z * 16, 16), 16), :] + VZ[1, 0:16, :]
    for s in range(4):
        YB[s] = own[4 * s : 4 * s + 4, :]
    cps = [send(YB.at[g], OB.at[q], S_GGRP + i, dev) for i, (g, dev) in enumerate(group)]
    OB[q] = YB[q]
    for cp in cps:
        cp.wait_recv()
    for s in range(4):
        oq_ref[:, s * IC : (s + 1) * IC] = OB[s]

    for cp in kcps:
        cp.wait_recv()
    for t in range(4):
        ok_ref[t * BLK : (t + 1) * BLK, :] = KG[t]
    for cp in started:
        if cp is not cpz:
            cp.wait_send()


def rows_in(v):
    return v.reshape(4, 2, 2, 16).transpose(0, 2, 1, 3).reshape(QN)


def per_device(
    main_query, index_query, index_weight, main_nope, main_rope, index_keys,
    query_pos, query_seg, key_pos, key_seg, loss_weight,
):
    mq = main_query.reshape(4, 4, 4, 2, QK)
    nope = mq[..., :DN].reshape(4, 4, 4, 2 * DN)
    rope = mq[..., DN:].reshape(4, 4, 4, 2 * DR)
    main = jnp.concatenate([nope, rope], axis=-1).reshape(4, 4, MC)
    wts = jnp.pad(index_weight.reshape(4, 4, 4), ((0, 0), (0, 0), (0, 124)))
    pack = jnp.concatenate([index_query.reshape(4, 4, IC), main, wts], axis=-1)
    pack = pack.transpose(1, 0, 2).astype(F32)
    zero = jnp.zeros_like(main_rope)
    rope2 = jnp.concatenate([main_rope, zero, zero, main_rope], axis=1)
    kcode = (key_seg * 65536 + key_pos)[:, None]
    qlow = rows_in(query_seg * 65536)
    qhigh = rows_in(query_seg * 65536 + query_pos)
    qv = jnp.stack([qlow, qhigh] + [qlow] * 6)
    lw = jnp.broadcast_to(rows_in(loss_weight)[None], (8, QN))

    vm = pltpu.VMEM
    scratch = [
        pltpu.SemaphoreType.DMA((N_SEM,)),
        pltpu.SemaphoreType.DMA((N_SEM,)),
        pltpu.SemaphoreType.DMA((4,)),
        vm((4, 4, CW), F32),
        vm((16, CW), F32),
        vm((4, QN, CW), BF16),
        vm((KEYS, HEADS * DN), BF16),
        vm((KEYS, QN), F32),
        vm((4, 8, QN), F32),
        vm((DI, KEYS), BF16),
        vm((4, BLK, QN), F32),
        vm((3, BLK, QN), F32),
        vm((BLK, QN), F32),
        vm((8, QN), F32),
        vm((3, 8, QN), F32),
        vm((HEADS, KEYS, QN), BF16),
        vm((4, HEADS, QN), F32),
        vm((4, HEADS, QN), F32),
        vm((5, HEADS + 8, QN), F32),
        vm((HEADS + 8, QN), F32),
        vm((3, HEADS + 8, QN), F32),
        vm((3, HEADS + 8, QN), F32),
        vm((HEADS + 8, QN), F32),
        vm((4, BLK, QN), BF16),
        vm((3, BLK, QN), BF16),
        vm((BLK, QN), F32),
        vm((4, BLK, QN), BF16),
        vm((5, 8, QN), F32),
        vm((3, 8, QN), F32),
        vm((8, QN), F32),
        vm((3, 8, QN), F32),
        vm((3, 8, QN), F32),
        vm((8, QN), F32),
        vm((4, BLK, DI), F32),
        vm((4, BLK, DI), BF16),
        vm((3, BLK, DI), BF16),
        vm((4, BLK, DI), F32),
        vm((4, QN, IC), F32),
        vm((2, QN, IC), F32),
        vm((2, QN, IC), F32),
        vm((4, 32, IC), F32),
        vm((2, 4, 32, IC), F32),
        vm((4, 32, IC), F32),
        vm((3, 32, IC), F32),
        vm((2, 32, IC), F32),
        vm((4, 4, IC), F32),
        vm((4, 4, IC), F32),
    ]
    vspec = pl.BlockSpec(memory_space=pltpu.VMEM)
    index_query_grad, index_key_grad, loss = pl.pallas_call(
        kernel,
        out_shape=(
            jax.ShapeDtypeStruct((4, 4 * IC), F32),
            jax.ShapeDtypeStruct((KEYS, DI), F32),
            jax.ShapeDtypeStruct((8, QN), F32),
        ),
        in_specs=[vspec] * 6 + [pl.BlockSpec(memory_space=pl.ANY)],
        out_specs=(vspec, vspec, vspec),
        scratch_shapes=scratch,
        compiler_params=pltpu.CompilerParams(
            collective_id=0, has_side_effects=True, vmem_limit_bytes=58 * 1024 * 1024
        ),
    )(pack, index_keys, rope2, kcode, qv, lw, main_nope)
    full = loss[0].reshape(4, 2, 2, 16).transpose(0, 2, 1, 3).reshape(QN)
    share = QN // lax.axis_size("hg")
    query_loss = lax.dynamic_slice_in_dim(full, lax.axis_index("hg") * share, share, 0)
    return (index_query_grad, index_key_grad, query_loss)


def solution(mesh):
    return jax.shard_map(
        per_device,
        mesh=mesh,
        in_specs=(
            P("ctx", "hg"),
            P("ctx", "hg"),
            P("ctx", "hg"),
            P("ctx", "hg"),
            P("ctx", None),
            P("ctx", None),
            P(),
            P(),
            P("ctx"),
            P("ctx"),
            P(),
        ),
        out_specs=(P("ctx", "hg"), P("ctx", None), P("hg")),
        check_vma=False,
    )
```

time: 2430 us -> 166 us (0.07)
  blocking collectives: 1320 us -> 0 us
  waiting for transfers between devices: 964 us -> 0 us
  Pallas kernels: 0 us -> 150 us
  matrix products: 64.6 us -> 0 us
  other arithmetic: 37.7 us -> 3.8 us
    unnamed x6 -> x0, waiting for transfers between devices: 771 us -> none
    psum x2 -> x0, blocking collectives: 609 us -> none  [the longest x1 400 us: per_device(): total = lax.psum(local_total, 'ctx')]
    pmax x2 -> x0, blocking collectives: 591 us -> none  [the longest x1 390 us: per_device(): lax.pmax(local_peak.astype(jnp.bfloat16), 'ctx').astype(local_peak.dtype)]
    psum x2 -> x0, waiting for transfers between devices: 156 us -> none  [the longest x1 103 us: per_device(): prob_sum, logits = lax.psum((probs, logit_part), 'hg')]
    pallas_call x0 -> x1, Pallas kernels: none -> 150 us  [per_device(): pl.pallas_call(kernel, out_shape=(jax.ShapeDtypeStruct((4, 4 * IC), F32),...]
    all_gather x1 -> x0, blocking collectives: 121 us -> none  [per_device(): lax.all_gather(index_weight, 'ctx', axis=0, tiled=True)]
    dot_general x5 -> x0, matrix products: 64.6 us -> none  [the longest x1 23.2 us: per_device(): jnp.einsum('qhd,kd->hqk', shaped[:, :, DN:], main_rope, preferred_element...]
    all_gather x2 -> x0, waiting for transfers between devices: 37.7 us -> none  [the longest x1 37.7 us: per_device(): lax.all_gather(main_query, 'ctx', axis=0, tiled=True)]
  transfers between devices with their start and end apart: 5 -> 0, of which waited for: 4 -> 0; matrix products, arithmetic and copies ran while one was open for 1% -> 0% of each run, Pallas kernels for 0% -> 0%
where the time goes in v1:
time: 166 us
  Pallas kernels  150 us (90%)
  local copies, waits for them, and re-layouts  11.2 us (7%)
  other arithmetic  3.8 us (2%)
    pallas_call x1, Pallas kernels, per_device(): pl.pallas_call(kernel, out_shape=(jax.ShapeDtypeStruct((4, 4 * IC), F32),...  150 us
    unnamed x3, local copies, waits for them, and re-layouts  4.31 us

profile of v1, /device:TPU:1, one launch (start us, length us, event | category | flops | bytes accessed | tf_op | source)
XLA Modules:
  0.0 165.9 jit_solution(5901803290067115948)
XLA Ops:
  0.6 0.9 reshape.38
  1.6 0.1 reshape.48
  1.8 0.8 reshape.42
  2.6 1.4 convert_bitcast_fusion.pack_ref
  4.0 0.7 fusion.2
  4.7 0.1 reshape.43
  4.8 0.1 stack_reshape.4
  4.9 0.1 reshape.44
  5.0 0.1 stack_reshape.5
  5.1 0.6 stack.3.qv_ref
  5.7 1.1 copy.31
  6.9 1.0 pad_maximum_fusion.rope_ref
  7.8 0.7 multiply_add_fusion
  8.5 1.0 copy.36.kcode_ref
  9.6 0.8 reshape.45
  10.3 0.1 broadcast_in_dim.11
  10.4 0.6 broadcast_in_dim.12.lw_ref
  11.0 150.1 %shard_map.130 = (f32[4,2048]{1,0:T(4,128)}, f32[1024,128]{1,0:T(8,128)}, f32[8,256]{1,0:T(8,128)}) custom-call(f32[4,4,2176]{2,1,0:T(4,128)} %convert_bitcast_fusion.pack_ref, bf16[1024,128]{1,0:T(8,128)(2,1)} %ik_ref.1, bf16[1024,256]{1,0:T(8,128)(2,1)} %pad_maximum_fusion.rope_ref, s32[1024,1]{1,0:T(8,128)} %copy.36.kcode_ref, s32[8,256]{1,0:T(8,128)} %stack.3.qv_ref, ...), custom_call_target="tpu_custom_call" | custom-call | tf_op jit(solution)/shard_map/pallas_call | solution.py:510
  161.2 0.7 slice_reduce_fusion
  161.9 0.1 reshape_squeeze.3
  162.0 0.1 reshape.46
  162.1 0.6 dynamic_slice.3
  162.7 1.4 copy.46
  164.0 1.9 %copy.47 = f32[1024,128]{1,0:T(8,128)} copy(f32[1024,128]{1,0:T(8,128)} %get-tuple-element.15) | data formatting | bytes 1048576
  (13 shorter events, 0.3 us)

commit v2 on v0

v2 whole, which is shorter than its diff:
```python
import functools
import math

import jax
import jax.numpy as jnp
from jax import lax
from jax.experimental import pallas as pl
from jax.experimental.pallas import tpu as pltpu
from jax.sharding import PartitionSpec as P

MESH = pl.DeviceIdType.MESH
F32 = jnp.float32
BF16 = jnp.bfloat16
DN = 128
DI = 128
QK = 192
PAIR = 2 * QK
H = 128
QN = 256
KEYS = 1024
BLK = 256
IC = 512
IW = IC + 128
MW = 2 * PAIR
HEADS = 32
HALF = HEADS // 2
G0 = HALF
LOG2E = math.log2(math.e)
NEG = -1e30
RING = (1, -1, 2)

S_AI, S_AM = 0, 7
S_WAVE = (14, 45, 76)
S_LOGIT, S_LNH, S_PROB, S_DL, S_CH = 107, 110, 113, 119, 125
S_LSE0, S_LSE1, S_LN, S_CR = 128, 136, 144, 161
S_KRS, S_KAG, S_GSIB, S_GPL, S_GFIN = 172, 178, 184, 186, 201
N_SEM = 208


def dot_tt(a, b):
    return lax.dot_general(a, b, (((1,), (1,)), ((), ())), preferred_element_type=F32)


def dot_nn(a, b):
    return lax.dot_general(a, b, (((1,), (0,)), ((), ())), preferred_element_type=F32)


def lse(parts):
    top = functools.reduce(jnp.maximum, parts)
    tot = functools.reduce(jnp.add, [jnp.exp2(v - top) for v in parts])
    return top + jnp.log2(tot)


def add(parts):
    return functools.reduce(jnp.add, parts)


def swap_rows(v):
    lane = lax.rem(lax.broadcasted_iota(jnp.int32, v.shape, 1), 64)
    up = pltpu.roll(v, QN - 16, 1)
    down = pltpu.roll(v, 16, 1)
    v = jnp.where((lane >= 16) & (lane < 32), up, v)
    return jnp.where((lane >= 32) & (lane < 48), down, v)


def kernel(
    mq_ref, iq_ref, iw_ref, rope_ref, ik_ref, kp_ref, ks_ref, qp_ref, qs_ref, lw_ref, nope_hbm,
    OB, KG, oloss_ref,
    ssem, rsem, lsem,
    FI, FM, SI, SM, RI, RM, XI, XM, AI, AM, GI, GM0, GM1, KV, ROPE, bias, W, LW, KT,
    L, LB, LNH, LNB,
    E, M, SUM, ES0, ES1, ESN, ESC, EB0, EB1, EBN, EBC, CH, CHB, PS, PB, PF, LQ, DL,
    KA, KS, KB, TT, T, RB, UB, VB, YB,
):
    me = lax.axis_index("ctx")
    hg = lax.axis_index("hg")
    c = lax.rem(me, 2)
    x = lax.rem(me // 2, 4)
    z = lax.rem(me // 8, 2)
    y = me // 16
    xb, xp = lax.rem(x, 2), x // 2
    q = xb * 2 + c
    slot = z * 4 + q
    first = c == 0

    def cid(yy, zz, xx, cc):
        return ((yy * 2 + zz) * 4 + xx) * 2 + cc

    def mod4(v):
        return lax.rem(v + 4, 4)

    octet = []
    for d in range(1, 8):
        cc = 1 - c if d % 2 else c
        bb = 1 - xb if d // 2 % 2 else xb
        zz = 1 - z if d // 4 else z
        octet.append((bb * 2 + cc, zz * 4 + bb * 2 + cc, (cid(y, zz, xp * 2 + bb, cc), hg)))
    sib = octet[0][2]
    zdev = octet[3][2]
    xdev = {s: (cid(y, z, mod4(x + s), c), hg) for s in RING}
    ydev = {s: (cid(mod4(y + s), z, x, c), hg) for s in RING}
    plane = {
        (dx, dy): (cid(mod4(y + dy), z, mod4(x + dx), c), hg)
        for dx in range(4) for dy in range(4) if (dx, dy) != (0, 0)
    }
    hdev = {s: (me, mod4(hg + s)) for s in (-3, -2, -1, 1, 2, 3)}
    r1 = {s: (jnp.where(first, xdev[s][0], ydev[s][0]), hg) for s in RING}
    r2 = {s: (jnp.where(first, ydev[s][0], xdev[s][0]), hg) for s in RING}

    started = []

    def send(src, dst, k, dev):
        cp = pltpu.make_async_remote_copy(
            src_ref=src, dst_ref=dst, send_sem=ssem.at[k], recv_sem=rsem.at[k],
            device_id=dev, device_id_type=MESH,
        )
        cp.start()
        started.append(cp)
        return cp

    loads = []
    for i in range(4):
        cols = pl.ds(i * 1024, 1024)
        cp = pltpu.make_async_copy(nope_hbm.at[:, cols], KV.at[:, cols], lsem.at[i])
        cp.start()
        loads.append(cp)

    barrier = pltpu.get_barrier_semaphore()
    partners = [dev for _, _, dev in octet if dev is not octet[1][2]]
    partners += list(plane.values()) + [hdev[s] for s in (1, 2, 3)]
    for dev in partners:
        pl.semaphore_signal(barrier, inc=1, device_id=dev, device_id_type=MESH)

    low = lax.broadcasted_iota(jnp.int32, (16, 128), 1) < 64
    FI[...] = jnp.zeros(FI.shape, F32)
    FI[16:20, 0:16] = iw_ref[...].astype(F32)
    for ch in range(4):
        for j in range(4):
            col = (ch * 4 + j) * DI
            FI[4 * j : 4 * j + 4, :] = iq_ref[:, col : col + DI].astype(F32)
        SI[ch] = FI[...].astype(BF16)
    pl.semaphore_wait(barrier, len(partners))

    a_i = [send(SI.at[g], RI.at[slot], S_AI + i, dev) for i, (g, _, dev) in enumerate(octet)]
    for ch in range(4):
        for p in range(4):
            col = (ch * 4 + p) * PAIR
            FM[4 * p : 4 * p + 4, :] = mq_ref[:, col : col + PAIR].astype(F32)
        t1, t2 = FM[:, 128:256], FM[:, 256:384]
        SM[ch, :, 0:128] = FM[:, 0:128].astype(BF16)
        SM[ch, :, 128:256] = jnp.where(
            low, pltpu.roll(t1, 64, 1), pltpu.roll(t2, 64, 1)
        ).astype(BF16)
        SM[ch, :, 256:384] = jnp.where(low, t1, t2).astype(BF16)
    a_m = [send(SM.at[g], RM.at[slot], S_AM + i, dev) for i, (g, _, dev) in enumerate(octet)]
    RI[slot] = SI[q]
    RM[slot] = SM[q]
    rows32 = pl.ds(pl.multiple_of((y * 2 + xp) * 32, 32), 32)
    for cp in a_i:
        cp.wait_recv()
    XI[...] = RI[...].astype(F32)
    for s in range(8):
        for j in range(5):
            AI[4 * s : 4 * s + 4, j * DI : (j + 1) * DI] = XI[s, 4 * j : 4 * j + 4, :]
    GI[q, rows32, :] = AI[...].astype(BF16)

    def r1_coord(s):
        xx, yy = mod4(x + s), mod4(y + s)
        return (
            jnp.where(first, lax.rem(xx, 2) * 2 + c, q),
            jnp.where(first, y, yy),
            jnp.where(first, xx // 2, xp),
        )

    def r2_coord(s, k):
        xx = jnp.where(first, mod4(x + k), mod4(x + s))
        yy = jnp.where(first, mod4(y + s), mod4(y + k))
        return (lax.rem(xx, 2) * 2 + c, yy, xx // 2)

    offs = (0, -1, 1, 2)

    def wave(G, base):
        s_r1, s_r2, s_sib = base, base + 3, base + 15
        sibs, one, two = [], {}, {}

        def unit(co):
            ch, yy, xx = co
            return G.at[ch, pl.ds(pl.multiple_of((yy * 2 + xx) * 32, 32), 32), :]

        def to_sib(co):
            u = unit(co)
            sibs.append(send(u, u, s_sib + len(sibs), sib))

        def to_two(k):
            u = unit(r1_coord(offs[k]))
            for i, s in enumerate(RING):
                two[s, k] = send(u, u, s_r2 + 3 * k + i, r2[s])

        u0 = unit(r1_coord(0))
        for i, s in enumerate(RING):
            one[s] = send(u0, u0, s_r1 + i, r1[s])
        to_sib(r1_coord(0))
        yield
        to_two(0)
        for k, s in ((1, 1), (2, -1), (3, 2)):
            one[s].wait_recv()
            to_two(k)
            to_sib(r1_coord(offs[k]))
        yield
        for s in RING:
            for k in range(4):
                two[s, k].wait_recv()
                to_sib(r2_coord(-s, offs[k]))
        yield
        for cp in sibs:
            cp.wait_recv()
        yield

    w_i = wave(GI, S_WAVE[0])
    next(w_i)
    for cp in a_m:
        cp.wait_recv()
    XM[...] = RM[...].astype(F32)
    for s in range(8):
        for p in range(4):
            AM[4 * s : 4 * s + 4, p * PAIR : (p + 1) * PAIR] = XM[s, 4 * p : 4 * p + 4, :]
    GM0[q, rows32, :] = AM[:, 0:MW].astype(BF16)
    GM1[q, rows32, :] = AM[:, MW : 2 * MW].astype(BF16)
    w_0 = wave(GM0, S_WAVE[1])
    w_1 = wave(GM1, S_WAVE[2])
    next(w_0)
    next(w_1)

    kcode = (ks_ref[...] * 65536 + kp_ref[...]).astype(F32)
    qcode = jnp.broadcast_to(qs_ref[...] * 65536, (8, QN)).astype(F32)
    qlow = swap_rows(qcode)[0:1, :]
    qhigh = swap_rows(qcode + jnp.broadcast_to(qp_ref[...], (8, QN)).astype(F32))[0:1, :]
    LW[...] = swap_rows(jnp.broadcast_to(lw_ref[...], (8, QN)))
    for r in range(8):
        col = jnp.transpose(jnp.broadcast_to(kcode[r : r + 1, :], (128, 128)))
        col = jnp.concatenate([col, col], axis=1)
        ok = (col >= qlow) & (col <= qhigh)
        bias[r * 128 : (r + 1) * 128, :] = jnp.where(ok, 0.0, NEG).astype(F32)
    next(w_i)
    next(w_0)
    next(w_1)
    for b in range(4):
        KT[b] = jnp.transpose(ik_ref[b * BLK : (b + 1) * BLK, :].astype(F32)).astype(BF16)
    rope = rope_ref[...].astype(F32)
    zero = jnp.zeros_like(rope)
    ROPE[:, 0:128] = jnp.transpose(jnp.concatenate([rope, zero], axis=0)).astype(BF16)
    ROPE[:, 128:256] = jnp.transpose(jnp.concatenate([zero, rope], axis=0)).astype(BF16)
    next(w_i)
    next(w_i)

    W[...] = jnp.transpose(GI[0, :, IC:IW].astype(F32))[0:16, :] * (1.0 / math.sqrt(DI))

    def index_part(t):
        trows = pl.ds(pl.multiple_of(t * BLK, BLK), BLK)
        L[t] = jnp.zeros((BLK, QN), F32)

        def chunk(ch, carry):
            acc = L[t]
            for j in range(4):
                d = dot_tt(ik_ref[trows, :], GI[ch, :, j * DI : (j + 1) * DI])
                acc = acc + jnp.maximum(d, 0.0) * W[pl.ds(4 * ch + j, 1), :]
            L[t] = acc
            return carry

        lax.fori_loop(0, 4, chunk, 0)

    lcps = []
    for s in (2, 1, 3):
        t = mod4(hg + s)
        index_part(t)
        lcps.append(send(L.at[t], LB.at[s - 1], S_LOGIT + s - 1, hdev[s]))
    index_part(hg)
    next(w_0)
    for cp in loads:
        cp.wait()
    next(w_0)

    scale = LOG2E / math.sqrt(QK)

    def main_pair(G, w, p, carry):
        ch = p // 2
        off = lax.rem(p, 2) * PAIR
        qr = G[ch, :, pl.ds(pl.multiple_of(off + 256, 128), 128)]
        for i in range(2):
            hd = w * HALF + 2 * p + i
            qn = G[ch, :, pl.ds(pl.multiple_of(off + i * 128, 128), 128)]
            rhs = jnp.concatenate([qn, qr], axis=1)
            kcols = pl.ds(pl.multiple_of((ch * 8 + w * 4 + lax.rem(p, 2) * 2 + i) * DN, 128), DN)
            for b in range(4):
                rows = slice(b * BLK, (b + 1) * BLK)
                lhs = jnp.concatenate(
                    [KV[rows, kcols], ROPE[rows, i * 128 : (i + 1) * 128]], axis=1
                )
                s = dot_tt(lhs, rhs) * scale + bias[rows, :]
                m = jnp.max(s, axis=0, keepdims=True)
                e = jnp.exp2(s - m)
                M[b, pl.ds(hd, 1), :] = m
                SUM[b, pl.ds(hd, 1), :] = jnp.sum(e, axis=0, keepdims=True)
                E[hd, rows, :] = e.astype(BF16)
        return carry

    pair0 = functools.partial(main_pair, GM0, 0)
    pair1 = functools.partial(main_pair, GM1, 1)

    def local_lse(a, b):
        r = slice(a, b)
        mm = functools.reduce(jnp.maximum, [M[i, r, :] for i in range(4)])
        ss = add([SUM[i, r, :] * jnp.exp2(M[i, r, :] - mm) for i in range(4)])
        return mm + jnp.log2(ss)

    def reduce_plane(S, B, base, combine):
        cp = send(S.at[0], B.at[0], base, sib)
        yield
        cp.wait_recv()
        S[1] = combine([S[0], B[0]])
        cps = [send(S.at[1], B.at[1 + i], base + 1 + i, dev) for i, dev in enumerate(plane.values())]
        yield
        for cp in cps:
            cp.wait_recv()
        S[3] = combine([S[1]] + [B[1 + i] for i in range(15)])
        cp = send(S.at[3], B.at[16], base + 16, zdev)
        yield
        cp.wait_recv()
        S[4] = combine([S[3], B[16]])
        yield

    def reduce_ctx(S, B, base, combine):
        cp = send(S.at[0], B.at[0], base, sib)
        yield
        cp.wait_recv()
        S[1] = combine([S[0], B[0]])
        cps = [send(S.at[1], B.at[1 + i], base + 1 + i, xdev[s]) for i, s in enumerate(RING)]
        yield
        for cp in cps:
            cp.wait_recv()
        S[2] = combine([S[1], B[1], B[2], B[3]])
        cps = [send(S.at[2], B.at[4 + i], base + 4 + i, ydev[s]) for i, s in enumerate(RING)]
        yield
        for cp in cps:
            cp.wait_recv()
        S[3] = combine([S[2], B[4], B[5], B[6]])
        cp = send(S.at[3], B.at[7], base + 7, zdev)
        yield
        cp.wait_recv()
        S[4] = combine([S[3], B[7]])
        yield

    lax.fori_loop(0, 6, pair0, 0)
    next(w_1)
    lax.fori_loop(6, 8, pair0, 0)
    ES0[0] = local_lse(0, G0)
    e_0 = reduce_ctx(ES0, EB0, S_LSE0, lse)
    next(e_0)
    next(w_1)
    lax.fori_loop(0, 6, pair1, 0)
    next(e_0)
    lax.fori_loop(6, 8, pair1, 0)
    ES1[0] = local_lse(G0, HEADS)
    e_1 = reduce_ctx(ES1, EB1, S_LSE1, lse)
    next(e_1)
    next(e_1)
    next(e_0)
    next(e_1)
    next(e_0)
    next(e_1)

    for cp in lcps:
        cp.wait_recv()
    lq = L[hg] + LB[0] + LB[1] + LB[2]
    LQ[...] = lq
    qrows = pl.ds(pl.multiple_of(hg * BLK, BLK), BLK)
    l2 = lq * LOG2E + bias[qrows, :]
    m = jnp.max(l2, axis=0, keepdims=True)
    part = m + jnp.log2(jnp.sum(jnp.exp2(l2 - m), axis=0, keepdims=True))
    LNH[...] = jnp.broadcast_to(part, (8, QN))
    ncps = [send(LNH, LNB.at[s - 1], S_LNH + s - 1, hdev[s]) for s in (1, 2, 3)]
    next(e_0)

    def head_sum(t, rows, n, acc, h0, h1):
        krows = pl.ds(pl.multiple_of(t * BLK + rows, 64), n)
        for hd in range(h0, h1):
            acc = acc + E[hd, krows, :].astype(F32) * M[t, hd : hd + 1, :]
        return acc

    for b in range(4):
        M[b, 0:G0, :] = jnp.exp2(M[b, 0:G0, :] - ES0[4])

    def sum_0(i, carry):
        t, rows = i // 4, lax.rem(i, 4) * 64
        PF[t, pl.ds(pl.multiple_of(rows, 64), 64), :] = head_sum(
            t, rows, 64, jnp.zeros((64, QN), F32), 0, G0
        )
        return carry

    lax.fori_loop(0, 16, sum_0, 0)
    for cp in ncps:
        cp.wait_recv()
    ESN[0] = lse([LNH[...], LNB[0], LNB[1], LNB[2]])
    e_n = reduce_plane(ESN, EBN, S_LN, lse)
    next(e_n)
    next(e_1)
    for b in range(4):
        M[b, G0:HEADS, :] = jnp.exp2(M[b, G0:HEADS, :] - ES1[4])

    def sum_1(t, u, own):
        def sub(i, carry):
            rows = u * 128 + i * 64
            here = pl.ds(pl.multiple_of(rows, 64), 64)
            acc = head_sum(t, rows, 64, PF[t, here, :], G0, HEADS)
            if own:
                PF[t, here, :] = acc
            else:
                PS[t, here, :] = acc.astype(BF16)
            return carry

        lax.fori_loop(0, 2, sub, 0)

    pcps = {}
    for u in range(2):
        part = slice(u * 128, (u + 1) * 128)
        for s in (2, 1, 3):
            t = mod4(hg + s)
            sum_1(t, u, False)
            pcps[u, s] = send(
                PS.at[t, part], PB.at[s - 1, part], S_PROB + 3 * u + s - 1, hdev[s]
            )
        if u == 0:
            next(e_n)
    for u in range(2):
        sum_1(hg, u, True)
    next(e_n)
    next(e_n)

    half = [slice(0, 128), slice(128, 256)]

    def grad_part(n, t, u, chunks):
        trows = pl.ds(pl.multiple_of(t * BLK + u * 128, 128), 128)

        def chunk(ch):
            qs = jnp.concatenate([GI[ch, :, j * DI : (j + 1) * DI] for j in range(4)], axis=0)
            d = dot_tt(ik_ref[trows, :], qs)
            dl = DL[t, half[u], :].astype(F32)
            ds = jnp.concatenate([
                jnp.where(
                    d[:, j * QN : (j + 1) * QN] > 0, dl * W[pl.ds(ch * 4 + j, 1), :], 0.0
                ).astype(BF16)
                for j in range(4)
            ], axis=1)
            KA[n, half[u], :] = KA[n, half[u], :] + dot_nn(ds, qs)
            tt = dot_nn(KT[t, :, half[u]], ds)
            if (n, u) == (0, 0):
                TT[ch] = tt
            elif (n, u) != (3, 1):
                TT[ch] = TT[ch] + tt
            else:
                tt = TT[ch] + tt
                for j in range(4):
                    T[ch, :, j * DI : (j + 1) * DI] = jnp.transpose(tt[:, j * QN : (j + 1) * QN])

        for ch in chunks:
            chunk(ch)

    KA[...] = jnp.zeros(KA.shape, F32)
    dcps = {}
    cross = jnp.zeros((1, QN), F32)
    for u in range(2):
        for s in (2, 1, 3):
            pcps[u, s].wait_recv()
        target = add([PF[hg, half[u], :]] + [PB[i, half[u], :].astype(F32) for i in range(3)])
        target = target * (1.0 / H)
        lq = LQ[half[u], :]
        brows = pl.ds(pl.multiple_of(hg * BLK + u * 128, 128), 128)
        prob = jnp.exp2(lq * LOG2E + bias[brows, :] - ESN[4, 0:1, :])
        DL[hg, half[u], :] = (LW[0:1, :] * (prob - target)).astype(BF16)
        for s in (2, 1, 3):
            mine = DL.at[hg, half[u]]
            dcps[u, s] = send(mine, mine, S_DL + 3 * u + s - 1, hdev[s])
        cross = cross + jnp.sum(target * lq, axis=0, keepdims=True)
        if u == 1:
            CH[...] = jnp.broadcast_to(cross, (8, QN))
            ccps = [send(CH, CHB.at[s - 1], S_CH + s - 1, hdev[s]) for s in (1, 2, 3)]
        grad_part(0, hg, u, range(4))

    kcps = {}
    order = (2, 1, 3)

    def key_out(n, u):
        KS[n - 1, half[u], :] = KA[n, half[u], :].astype(BF16)
        kcps[n, u] = send(
            KS.at[n - 1, half[u]], KB.at[n - 1, half[u]], S_KRS + 3 * u + n - 1, hdev[-order[n - 1]]
        )

    def key_sum(u):
        for n in (1, 2, 3):
            kcps[n, u].wait_recv()
        tot = KA[0, half[u], :] + add([KB[i, half[u], :].astype(F32) for i in range(3)])
        KG[hg, half[u], :] = tot.astype(BF16)
        mine = KG.at[hg, half[u]]
        return [send(mine, mine, S_KAG + 3 * u + s - 1, hdev[s]) for s in (2, 1, 3)]

    for u in range(2):
        for n in (1, 2, 3):
            if (n, u) == (3, 1):
                continue
            dcps[u, order[n - 1]].wait_recv()
            grad_part(n, mod4(hg - order[n - 1]), u, range(4))
            key_out(n, u)
            if (n, u) == (1, 1):
                next(e_c)
        if u == 0:
            for cp in ccps:
                cp.wait_recv()
            ESC[0] = add([CH[...], CHB[0], CHB[1], CHB[2]])
            e_c = reduce_ctx(ESC, EBC, S_CR, add)
            next(e_c)
    next(e_c)
    dcps[1, order[2]].wait_recv()

    turns = (1 - xb, xb)
    gcps = []
    for i, k in enumerate(turns):
        grad_part(3, mod4(hg - order[2]), 1, (2 * k, 2 * k + 1))
        gcps.append(send(T.at[2 * k + 1 - c], RB.at[k], S_GSIB + i, sib))
    key_out(3, 1)
    vcps = []
    for i, k in enumerate(turns):
        gcps[i].wait_recv()
        UB[k] = (T[2 * k + c] + RB[k]).astype(BF16)
        for dx in ((1, 3), (0, 2))[i]:
            for dy in (0, 1, 3, 2):
                if (dx, dy) == (0, 0):
                    continue
                n = dx * 4 + dy - 1
                xx, yy = mod4(x + dx), mod4(y + dy)
                urows = pl.ds(pl.multiple_of((yy * 2 + xx // 2) * 32, 32), 32)
                vcps.append(send(UB.at[k, urows], VB.at[n], S_GPL + n, plane[dx, dy]))
    own = T[q, rows32, :] + RB[xb, rows32, :]
    gkcps = key_sum(0)
    next(e_c)
    gkcps += key_sum(1)

    for cp in vcps:
        cp.wait_recv()
    own = own + add([VB[i].astype(F32) for i in range(15)])
    for s in range(8):
        YB[s] = own[4 * s : 4 * s + 4, :]
    cps = [
        send(YB.at[g], OB.at[slot], S_GFIN + i, dev) for i, (_, g, dev) in enumerate(octet)
    ]
    OB[slot] = YB[slot]
    next(e_c)
    loss = LW[...] * (ESN[4] * (1.0 / LOG2E) - ESC[4])
    oloss_ref[...] = pltpu.roll(swap_rows(loss), lax.rem(QN - 64 * hg, QN), 1)
    for cp in cps + gkcps:
        cp.wait_recv()
    for cp in started:
        cp.wait_send()


def finish(ob_ref, kg_ref, loss_ref, oq_ref, ok_ref, oloss_ref):
    for s in range(4):
        oq_ref[:, s * IC : (s + 1) * IC] = ob_ref[s] + ob_ref[4 + s]
    for t in range(4):
        ok_ref[t * BLK : (t + 1) * BLK, :] = kg_ref[t].astype(F32)
    oloss_ref[...] = loss_ref[0:1, 0:64]


def per_device(
    main_query, index_query, index_weight, main_nope, main_rope, index_keys,
    query_pos, query_seg, key_pos, key_seg, loss_weight,
):
    vm = pltpu.VMEM
    scratch = [
        pltpu.SemaphoreType.DMA((N_SEM,)),
        pltpu.SemaphoreType.DMA((N_SEM,)),
        pltpu.SemaphoreType.DMA((4,)),
        vm((32, DI), F32),
        vm((16, PAIR), F32),
        vm((4, 32, DI), BF16),
        vm((4, 16, PAIR), BF16),
        vm((8, 32, DI), BF16),
        vm((8, 16, PAIR), BF16),
        vm((8, 32, DI), F32),
        vm((8, 16, PAIR), F32),
        vm((32, IW), F32),
        vm((32, 2 * MW), F32),
        vm((4, QN, IW), BF16),
        vm((4, QN, MW), BF16),
        vm((4, QN, MW), BF16),
        vm((KEYS, HEADS * DN), BF16),
        vm((KEYS, 256), BF16),
        vm((KEYS, QN), F32),
        vm((16, QN), F32),
        vm((8, QN), F32),
        vm((4, DI, BLK), BF16),
        vm((4, BLK, QN), F32),
        vm((3, BLK, QN), F32),
        vm((8, QN), F32),
        vm((3, 8, QN), F32),
        vm((HEADS, KEYS, QN), BF16),
        vm((4, HEADS, QN), F32),
        vm((4, HEADS, QN), F32),
        vm((5, G0, QN), F32),
        vm((5, HEADS - G0, QN), F32),
        vm((5, 8, QN), F32),
        vm((5, 8, QN), F32),
        vm((8, G0, QN), F32),
        vm((8, HEADS - G0, QN), F32),
        vm((17, 8, QN), F32),
        vm((8, 8, QN), F32),
        vm((8, QN), F32),
        vm((3, 8, QN), F32),
        vm((4, BLK, QN), BF16),
        vm((3, BLK, QN), BF16),
        vm((4, BLK, QN), F32),
        vm((BLK, QN), F32),
        vm((4, BLK, QN), BF16),
        vm((4, BLK, DI), F32),
        vm((3, BLK, DI), BF16),
        vm((3, BLK, DI), BF16),
        vm((4, DI, 4 * QN), F32),
        vm((4, QN, IC), F32),
        vm((2, QN, IC), F32),
        vm((2, QN, IC), BF16),
        vm((15, 32, IC), BF16),
        vm((8, 4, IC), F32),
    ]
    vspec = pl.BlockSpec(memory_space=pltpu.VMEM)
    ob, kg, loss = pl.pallas_call(
        kernel,
        out_shape=(
            jax.ShapeDtypeStruct((8, 4, IC), F32),
            jax.ShapeDtypeStruct((4, BLK, DI), BF16),
            jax.ShapeDtypeStruct((8, QN), F32),
        ),
        in_specs=[vspec] * 10 + [pl.BlockSpec(memory_space=pl.ANY)],
        out_specs=(vspec, vspec, vspec),
        scratch_shapes=scratch,
        compiler_params=pltpu.CompilerParams(
            collective_id=0, has_side_effects=True, vmem_limit_bytes=58 * 1024 * 1024
        ),
    )(
        main_query, index_query, index_weight, main_rope.T, index_keys,
        key_pos.reshape(8, 128), key_seg.reshape(8, 128),
        query_pos.reshape(1, QN), query_seg.reshape(1, QN), loss_weight.reshape(1, QN),
        main_nope,
    )
    index_query_grad, index_key_grad, loss = pl.pallas_call(
        finish,
        out_shape=(
            jax.ShapeDtypeStruct((4, 4 * IC), F32),
            jax.ShapeDtypeStruct((KEYS, DI), F32),
            jax.ShapeDtypeStruct((1, 64), F32),
        ),
        in_specs=[vspec] * 3,
        out_specs=(vspec, vspec, vspec),
    )(ob, kg, loss)
    return (index_query_grad, index_key_grad, loss.reshape(64))


def solution(mesh):
    return jax.shard_map(
        per_device,
        mesh=mesh,
        in_specs=(
            P("ctx", "hg"),
            P("ctx", "hg"),
            P("ctx", "hg"),
            P("ctx", "hg"),
            P("ctx", None),
            P("ctx", None),
            P(),
            P(),
            P("ctx"),
            P("ctx"),
            P(),
        ),
        out_specs=(P("ctx", "hg"), P("ctx", None), P("hg")),
        check_vma=False,
    )
```

time: 2430 us -> 117 us (0.05)
  blocking collectives: 1320 us -> 0 us
  waiting for transfers between devices: 964 us -> 0 us
  Pallas kernels: 0 us -> 117 us
  matrix products: 64.6 us -> 0 us
  other arithmetic: 37.7 us -> 0 us
    unnamed x6 -> x0, waiting for transfers between devices: 771 us -> none
    psum x2 -> x0, blocking collectives: 609 us -> none  [the longest x1 400 us: per_device(): total = lax.psum(local_total, 'ctx')]
    pmax x2 -> x0, blocking collectives: 591 us -> none  [the longest x1 390 us: per_device(): lax.pmax(local_peak.astype(jnp.bfloat16), 'ctx').astype(local_peak.dtype)]
    psum x2 -> x0, waiting for transfers between devices: 156 us -> none  [the longest x1 103 us: per_device(): prob_sum, logits = lax.psum((probs, logit_part), 'hg')]
    all_gather x1 -> x0, blocking collectives: 121 us -> none  [per_device(): lax.all_gather(index_weight, 'ctx', axis=0, tiled=True)]
    pallas_call x0 -> x2, Pallas kernels: none -> 117 us  [the longest x1 115 us: per_device(): pl.pallas_call(kernel, out_shape=(jax.ShapeDtypeStruct((8, 4, IC), F32),...]
    dot_general x5 -> x0, matrix products: 64.6 us -> none  [the longest x1 23.2 us: per_device(): jnp.einsum('qhd,kd->hqk', shaped[:, :, DN:], main_rope, preferred_element...]
    all_gather x2 -> x0, waiting for transfers between devices: 37.7 us -> none  [the longest x1 37.7 us: per_device(): lax.all_gather(main_query, 'ctx', axis=0, tiled=True)]
  transfers between devices with their start and end apart: 5 -> 0, of which waited for: 4 -> 0; matrix products, arithmetic and copies ran while one was open for 1% -> 0% of each run, Pallas kernels for 0% -> 0%
where the time goes in v2:
time: 117 us
  Pallas kernels  117 us (100%)
    pallas_call x1, Pallas kernels, per_device(): pl.pallas_call(kernel, out_shape=(jax.ShapeDtypeStruct((8, 4, IC), F32),...  115 us

profile of v2, /device:TPU:1, one launch (start us, length us, event | category | flops | bytes accessed | tf_op | source)
XLA Modules:
  0.0 117.2 jit_solution(15292996128675985134)
XLA Ops:
  0.6 114.7 %shard_map.130 = (f32[8,4,512]{2,1,0:T(4,128)}, bf16[4,256,128]{2,1,0:T(8,128)(2,1)}, f32[8,256]{1,0:T(8,128)}) custom-call(bf16[4,6144]{1,0:T(4,128)(2,1)} %mq_ref.1, bf16[4,2048]{1,0:T(4,128)(2,1)} %iq_ref.1, bf16[4,16]{1,0:T(4,128)(2,1)} %iw_ref.1, bf16[64,1024]{1,0:T(8,128)(2,1)} %bitcast.7, bf16[1024,128]{1,0:T(8,128)(2,1)} %ik_ref.1, ...), custom_call_target="tpu_custom_call" | custom-call | tf_op jit(solution)/shard_map/pallas_call | solution.py:634
  115.4 1.8 %shard_map.131 = (f32[4,2048]{1,0:T(4,128)}, f32[1024,128]{1,0:T(8,128)}, f32[1,64]{1,0:T(1,128)}) custom-call(f32[8,4,512]{2,1,0:T(4,128)} %get-tuple-element.9.ob_ref, bf16[4,256,128]{2,1,0:T(8,128)(2,1)} %get-tuple-element.10.kg_ref, f32[8,256]{1,0:T(8,128)} %get-tuple-element.11.loss_ref), custom_call_target="tpu_custom_call" | custom-call | tf_op jit(solution)/shard_map/pallas_call | solution.py:653
